TPU v7x, 256 devices: a whole 4x4x8 slice. The times are simulated.
256 devices in a mesh: ctx: 32 (over y, x, core), head: 8 (over z).
Axes of the slice: x: 4, y: 4, z: 8, core: 2. Of those that a mesh axis runs over, the one named last changes fastest.
Arguments:
- queries: bfloat16 [16384, 4096], P('ctx', 'head'), may hold values from -6 to 6
- keys: bfloat16 [16384, 4096], P('ctx', 'head'), may hold values from -6 to 6
- values: bfloat16 [16384, 4096], P('ctx', 'head'), may hold values from -6 to 6
- log_decay: float32 [32, 16384], P('head', 'ctx'), may hold values from -2 to 0
- level_pick: int32 [32, 16384], P('head', 'ctx'), may hold values from 0 to 15
- level_table: float32 [32, 8, 16], P('head'), may hold values from 0.2 to 2
- out_weight: bfloat16 [4096, 8192], P('head', 'ctx'), may hold values from -0.1875 to 0.1875
Outputs:
- layer_out: bfloat16 [16384, 8192], P('ctx', 'head')
All inputs are finite; a program needn't handle non-finite values.
Results may differ from a plain program's by a relative error of at most 0.024.
Values may be sent and summed in bfloat16 or wider, within the bound.
A program may use at most 128 MiB of HBM per device.

v0:
```python
import jax
import jax.numpy as jnp
import numpy as np
from jax import lax
from jax.sharding import PartitionSpec as P

HD = 128
BLOCK = 128


def local(queries, keys, values, log_decay, level_pick, level_table, out_weight):
    token_count = queries.shape[0]
    head_count = log_decay.shape[0]
    block_count = token_count // BLOCK
    level_count = level_table.shape[1]
    table_size = level_table.shape[2]
    query_blocks = queries.reshape(block_count, BLOCK, head_count, HD)
    key_blocks = keys.reshape(block_count, BLOCK, head_count, HD)
    value_blocks = values.reshape(block_count, BLOCK, head_count, HD)
    within = jnp.cumsum(log_decay.reshape(head_count, block_count, BLOCK), axis=2)
    block_decay = within[:, :, -1]
    block_end = jnp.cumsum(block_decay, axis=1)
    block_start = block_end - block_decay
    one_hot = (
        level_pick[:, None, :] == lax.broadcasted_iota(jnp.int32, (1, table_size, 1), 1)
    ).astype(jnp.float32)
    level_weight = jnp.einsum("hlk,hkt->hlt", level_table, one_hot, precision=lax.Precision.HIGHEST)
    level_weight = level_weight.reshape(head_count, level_count, block_count, BLOCK)
    scores = jnp.einsum(
        "cthd,cshd->hcts", query_blocks, key_blocks, preferred_element_type=jnp.float32
    )
    rows = lax.broadcasted_iota(jnp.int32, (BLOCK, BLOCK), 0)
    cols = lax.broadcasted_iota(jnp.int32, (BLOCK, BLOCK), 1)
    causal = rows >= cols
    log_gaps = within[:, :, :, None] - within[:, :, None, :]
    decays = jnp.where(causal, jnp.exp(jnp.where(causal, log_gaps, 0.0)), 0.0)
    weights = (level_weight[:, 0, :, :, None] * decays * scores).astype(jnp.bfloat16)
    local_out = jnp.einsum(
        "hcts,cshd->hctd", weights, value_blocks, preferred_element_type=jnp.float32
    )
    scaled = jnp.exp(block_decay[:, :, None] - within)
    block_keys = (key_blocks * jnp.transpose(scaled, (1, 2, 0))[:, :, :, None]).astype(jnp.bfloat16)
    states = jnp.einsum(
        "cshd,cshe->hcde", block_keys, value_blocks, preferred_element_type=jnp.float32
    )
    level_list = []
    dev_bits = block_count.bit_length() - 1
    numbers = np.arange(block_count)
    for level in range(dev_bits):
        upper_end = numbers >> level << level
        bit_set = numbers >> level & 1 == 1
        inside = (
            bit_set[:, None]
            & (numbers[None, :] >= (upper_end - (1 << level))[:, None])
            & (numbers[None, :] < upper_end[:, None])
        )
        factors = jnp.where(
            jnp.asarray(inside)[None],
            jnp.exp(jnp.minimum(block_start[:, :, None] - block_end[:, None, :], 0.0)),
            0.0,
        )
        level_list.append(
            jnp.einsum("hcm,hmde->hcde", factors, states, precision=lax.Precision.HIGHEST)
        )
    summary = jnp.einsum(
        "hm,hmde->hde",
        jnp.exp(block_end[:, -1:] - block_end),
        states,
        precision=lax.Precision.HIGHEST,
    )
    total_decay = block_end[:, -1]
    ctx_bits = lax.axis_size("ctx").bit_length() - 1
    my_index = lax.axis_index("ctx")
    remote_list = []
    all_decay = lax.all_gather(total_decay[None, :], "ctx", axis=0, tiled=True)
    running_end = jnp.cumsum(all_decay, axis=0)
    own_start = lax.dynamic_index_in_dim(running_end - all_decay, my_index, 0, keepdims=False)
    bit_ids = jnp.arange(ctx_bits, dtype=jnp.int32)
    upper_dev = my_index >> bit_ids << bit_ids
    lower_dev = upper_dev - (1 << bit_ids)
    dev_set = my_index >> bit_ids & 1 == 1
    initial = jnp.zeros((ctx_bits, head_count, HD, HD), jnp.float32)
    block_rows = lax.all_gather(
        summary[None].astype(jnp.bfloat16), "ctx", axis=0, tiled=True
    ).astype(jnp.float32)
    row_count = block_rows.shape[0]
    device_ids = jnp.arange(row_count, dtype=jnp.int32)
    member = (
        dev_set[:, None]
        & (device_ids[None, :] >= lower_dev[:, None])
        & (device_ids[None, :] < upper_dev[:, None])
    )
    factors = jnp.where(
        member[:, :, None],
        jnp.exp(jnp.minimum(own_start[None, None, :] - running_end[None, :, :], 0.0)),
        0.0,
    )
    remote = initial + jnp.einsum(
        "jnh,nhde->jhde", factors, block_rows, precision=lax.Precision.HIGHEST
    )
    for level in range(ctx_bits):
        remote_list.append(remote[level])
    for remote_state in remote_list:
        level_list.append(jnp.exp(block_start)[:, :, None, None] * remote_state[:, None, :, :])
    level_total = len(level_list)
    stacked = jnp.concatenate(level_list, axis=2).astype(jnp.bfloat16)
    query_heads = jnp.transpose(query_blocks, (2, 0, 1, 3))
    level_queries = (
        level_weight[:, 1:, :, :, None]
        * jnp.exp(within)[:, None, :, :, None]
        * query_heads[:, None]
    )
    level_queries = (
        jnp.transpose(level_queries, (0, 2, 3, 1, 4))
        .reshape(head_count, block_count, BLOCK, level_total * HD)
        .astype(jnp.bfloat16)
    )
    readout = jnp.einsum(
        "hctk,hcke->hcte", level_queries, stacked, preferred_element_type=jnp.float32
    )
    mixture = local_out + readout
    normed = (
        mixture * lax.rsqrt(jnp.mean(mixture * mixture, axis=-1, keepdims=True) + 1e-06)
    ).astype(jnp.bfloat16)
    flattened = jnp.transpose(normed, (1, 2, 0, 3)).reshape(token_count, head_count * HD)
    projected = jnp.dot(
        flattened,
        lax.all_gather(out_weight, "ctx", axis=1, tiled=True),
        preferred_element_type=jnp.float32,
    )
    final_output = lax.psum_scatter(
        projected.astype(jnp.bfloat16), "head", scatter_dimension=1, tiled=True
    )
    return final_output


def solution(mesh):
    in_specs = (
        P("ctx", "head"),
        P("ctx", "head"),
        P("ctx", "head"),
        P("head", "ctx"),
        P("head", "ctx"),
        P("head", None, None),
        P("head", "ctx"),
    )
    out_specs = P("ctx", "head")
    return jax.shard_map(local, mesh=mesh, in_specs=in_specs, out_specs=out_specs, check_vma=False)
```

profile of v0, /device:TPU:1, one launch (start us, length us, event | category | flops | bytes accessed | tf_op | source)
XLA Modules:
  0.0 248.4 jit_solution(14025969505748591224)
XLA Ops:
  6.5 0.7 reshape.165
  7.3 1.2 reduce_window_sum.37
  9.2 1.2 reshape.167
  10.8 1.2 reshape.168
  12.3 2.4 fusion.17
  14.7 0.7 convert_element_type.45
  15.4 0.7 all-gather.5.cloned.1.call-update
  17.7 65.7 %all-reduce = f32[128]{0:T(128)S(1)} all-reduce(f32[128]{0:T(128)S(1)} %dynamic-update-slice), channel_id=3, replica_groups=mesh['ctx'=32,'head'=8] {'ctx'}, use_global_device_ids=true, to_apply=%add | all-reduce | flops 128 | bytes 1024
  84.9 3.2 %fusion.7 = bf16[4,4,896,128]{3,1,2,0:T(4,128)(2,1)} fusion(f32[4,4,128,128]{3,2,1,0:T(8,128)S(1)} %fusion.20, f32[4,4]{1,0:T(4,128)S(1)} %reduce_window_sum.38, f32[4,4]{1,0:T(4,128)S(1)} %subtract_reduce_fusion, pred[4,4]{1,0:T(4,128)(4,1)S(1)} %copy-done.7), kind=kOutput, calls=%fused_computation.11 | convolution fusion | flops 12845247 | bytes 1573008 | tf_op jit(solution)/shard_map/hcm,hmde->hcde/dot_general | solution.py:63
  88.1 3.2 %fusion.8 = bf16[4,4,896,128]{3,1,2,0:T(4,128)(2,1)} fusion(bf16[4,4,896,128]{3,1,2,0:T(4,128)(2,1)} %fusion.7, f32[4,4,128,128]{3,2,1,0:T(8,128)S(1)} %fusion.20, f32[4,4]{1,0:T(4,128)S(1)} %reduce_window_sum.38, f32[4,4]{1,0:T(4,128)S(1)} %subtract_reduce_fusion, pred[4,4]{1,0:T(4,128)(4,1)S(1)} %copy-done.5), kind=kOutput, calls=%fused_computation.12 | convolution fusion | flops 12845248 | bytes 1573008 | tf_op jit(solution)/shard_map/hcm,hmde->hcde/dot_general | solution.py:63
  91.3 2.9 %multiply_convert_fusion = bf16[4,4,128,7,128]{2,4,3,1,0:T(8,128)(2,1)} fusion(f32[4,4,128,128]{2,3,1,0:T(8,128)S(1)} %convert_bitcast_fusion, f32[4,4,128,7]{2,3,1,0:T(8,128)S(1)} %fusion.36), kind=kLoop, calls=%fused_computation.1 | loop fusion | flops 3670016 | bytes 4775936 | tf_op jit(solution)/shard_map/convert_element_type | solution.py:116
  94.2 6.6 %fusion.4 = f32[5,4,128,128]{3,0,2,1:T(8,128)S(1)} fusion(bf16[32,4,128,128]{3,2,1,0:T(8,128)(2,1)} %bitcast.65, f32[32,4]{0,1:T(4,128)S(1)} %copy.45, pred[5,32]{1,0:T(8,128)(4,1)S(1)} %fusion.55), kind=kOutput, calls=%fused_computation.6 | convolution fusion | flops 125829760 | bytes 5505696 | tf_op jit(solution)/shard_map/jnh,nhde->jhde/dot_general | solution.py:98
  100.8 1.2 fusion.63
  102.0 1.1 fusion.21
  103.1 1.1 fusion.22
  104.1 1.1 fusion.23
  105.2 1.0 fusion.24
  106.2 1.1 fusion.25
  107.3 3.4 %fusion.2 = f32[4,4,128,128]{2,3,1,0:T(8,128)S(1)} fusion(bf16[4,4,128,896]{2,3,1,0:T(8,128)(2,1)S(1)} %bitcast.64, bf16[4,4,896,128]{3,1,2,0:T(4,128)(2,1)} %fusion.25), kind=kOutput, calls=%fused_computation.4 | convolution fusion | flops 469762048 | bytes 8388608 | tf_op jit(solution)/shard_map/hctk,hcke->hcte/dot_general | solution.py:118
  110.7 2.1 multiply_reduce_fusion
  112.8 1.3 fusion.10
  114.5 22.9 %all-gather.5.cloned.1.call-done = bf16[512,8192]{1,0:T(8,128)(2,1)} async-done(((bf16[512,256]{1,0:T(8,128)(2,1)}), bf16[512,8192]{1,0:T(8,128)(2,1)}) %all-gather.5.cloned.1.call-update) | async-done | bytes 8388624 | tf_op jit(solution)/shard_map/all_gather | solution.py:128
  137.4 10.1 %convolution_convert_fusion = bf16[512,8192]{1,0:T(8,128)(2,1)} fusion(bf16[512,8192]{1,0:T(8,128)(2,1)} %all-gather.5.cloned.1.call-done, bf16[64,8,4,128]{3,2,1,0:T(4,128)(2,1)S(1)} %bitcast.72), kind=kOutput, calls=%fused_computation | convolution fusion | flops 4299161600 | bytes 17301504 | tf_op jit(solution)/shard_map/dot_general | solution.py:126
  147.4 94.5 %reduce-scatter.2.cloned.1.call-done = bf16[512,1024]{1,0:T(8,128)(2,1)} async-done(((bf16[512,8192]{1,0:T(8,128)(2,1)}), bf16[512,1024]{1,0:T(8,128)(2,1)}) %reduce-scatter.2.cloned.1.call-update) | async-done | bytes 1048592 | tf_op jit(solution)/shard_map/reduce_scatter | solution.py:131
  (53 shorter events, 4.1 us)
Async XLA Ops:
  6.5 77.8 %copy-start = (f32[4,8,16]{2,1,0:T(8,128)S(1)}, f32[4,8,16]{2,1,0:T(8,128)}, u32[]{:S(2)}) copy-start(f32[4,8,16]{2,1,0:T(8,128)} %param.14) | copy-start | bytes 6148
  6.5 87.7 %all-gather.7.cloned.1.call-start = ((), (), s32[]{:S(2)}) async-start(), calls=%async_computation.3 | async-start | bytes 4325376 | tf_op jit(solution)/shard_map/all_gather | solution.py:83
  9.1 7.1 %copy-start.6 = (u32[256]{0:T(256)S(1)}, u32[256]{0:T(256)}, u32[]{:S(2)}) copy-start(u32[256]{0:T(256)} %constant.43) | copy-start | bytes 3076
  9.2 74.6 %copy-start.2 = (bf16[512,512]{1,0:T(8,128)(2,1)S(1)}, bf16[512,512]{1,0:T(8,128)(2,1)}, u32[]{:S(2)}) copy-start(bf16[512,512]{1,0:T(8,128)(2,1)} %param.9) | copy-start | bytes 1572868
  10.8 73.5 %copy-start.4 = (s32[4,512]{1,0:T(4,128)S(1)}, s32[4,512]{1,0:T(4,128)}, u32[]{:S(2)}) copy-start(s32[4,512]{1,0:T(4,128)} %param.13) | copy-start | bytes 24580
  12.0 72.9 %copy-start.7 = (pred[4,4]{1,0:T(4,128)(4,1)S(1)}, pred[4,4]{1,0:T(4,128)(4,1)}, u32[]{:S(2)}) copy-start(pred[4,4]{1,0:T(4,128)(4,1)} %constant.36.clone) | copy-start | bytes 52
  14.7 73.4 %copy-start.5 = (pred[4,4]{1,0:T(4,128)(4,1)S(1)}, pred[4,4]{1,0:T(4,128)(4,1)}, u32[]{:S(2)}) copy-start(pred[4,4]{1,0:T(4,128)(4,1)} %constant.37.clone) | copy-start | bytes 52
  15.4 122.0 %all-gather.5.cloned.1.call-start = ((), (), s32[]{:S(2)}) async-start(), calls=%async_computation.1 | async-start | bytes 8650752 | tf_op jit(solution)/shard_map/all_gather | solution.py:128
  16.1 225.8 %reduce-scatter.2.cloned.1.call-start = ((), (), s32[]{:S(2)}) async-start(), calls=%async_computation.2 | async-start | bytes 9437184 | tf_op jit(solution)/shard_map/reduce_scatter | solution.py:131
  84.5 9.7 %copy-start.3 = (f32[4,8,4,128]{3,1,2,0:T(8,128)}, f32[4,8,4,128]{3,1,2,0:T(8,128)S(1)}, u32[]{:S(2)}) copy-start(f32[4,8,4,128]{3,1,2,0:T(8,128)S(1)} %convolution_bitcast_fusion) | copy-start | bytes 196612
  100.8 6.5 %copy-start.1 = (bf16[4,4,128,7,128]{2,4,3,1,0:T(8,128)(2,1)S(1)}, bf16[4,4,128,7,128]{2,4,3,1,0:T(8,128)(2,1)}, u32[]{:S(2)}) copy-start(bf16[4,4,128,7,128]{2,4,3,1,0:T(8,128)(2,1)} %multiply_convert_fusion) | copy-start | bytes 11010052
  107.3 3.4 %slice-start = ((f32[4,8,4,128]{3,1,2,0:T(8,128)}), f32[4,1,4,128]{3,1,2,0:T(1,128)S(1)}, s32[]{:S(2)}) async-start(f32[4,8,4,128]{3,1,2,0:T(8,128)} %copy-done.3), calls=%async_computation.4 | async-start | bytes 16384 | tf_op jit(solution)/shard_map/slice | solution.py:37
Sparse Core Ops, SparseCore 0:
  15.5 55.3 all-gather.6
  73.4 63.9 all-gather.4
  147.6 94.2 reduce-scatter.1
where the time goes:
time: 249 us; the launch traced here: 248 us
  waiting for transfers between devices  118 us (47%)
  blocking collectives  65.7 us (26%)
  matrix products  31.3 us (13%)
  between operations  14 us (6%)
  other arithmetic  12.2 us (5%)
  local copies, waits for them, and re-layouts  7.04 us (3%)
    reduce_scatter x1, waiting for transfers between devices, local(): lax.psum_scatter(projected.astype(jnp.bfloat16), 'head', scatter_dimensio...  94.5 us
    unnamed x1, blocking collectives  65.7 us
    all_gather x1, waiting for transfers between devices, local(): lax.all_gather(out_weight, 'ctx', axis=1, tiled=True)  22.9 us
    dot_general x1, matrix products, local(): jnp.dot(flattened, lax.all_gather(out_weight, 'ctx', axis=1, tiled=True),...  10.1 us
    dot_general x1, matrix products, local(): jnp.einsum('jnh,nhde->jhde', factors, block_rows, precision=lax.Precision...  6.6 us
    dot_general x2, matrix products, local(): jnp.einsum('hcm,hmde->hcde', factors, states, precision=lax.Precision.HIG...  6.35 us
  transfers between devices with their start and end apart: 3, of which 2 were waited for; matrix products, arithmetic and copies ran while one was open for 13% of the time, Pallas kernels for 0%

commit v1 on v0

--- a/solution.py
+++ b/solution.py
@@ -125,7 +125,9 @@
     flattened = jnp.transpose(normed, (1, 2, 0, 3)).reshape(token_count, head_count * HD)
     projected = jnp.dot(
         flattened,
-        lax.all_gather(out_weight, "ctx", axis=1, tiled=True),
+        jnp.concatenate(
+            lax.all_to_all(jnp.stack([out_weight] * lax.axis_size("ctx")), "ctx", 0, 0), axis=1
+        ),
         preferred_element_type=jnp.float32,
     )
     final_output = lax.psum_scatter(

time: 249 us -> 334 us (1.34)
  blocking collectives: 65.7 us -> 162 us
  waiting for transfers between devices: 118 us -> 93.1 us
  starting transfers between devices: 0.08 us -> 8.82 us
  local copies, waits for them, and re-layouts: 7.04 us -> 11.3 us
    unnamed x1, blocking collectives: 65.7 us -> 162 us
    all_gather x1 -> x0, waiting for transfers between devices: 22.9 us -> none  [local(): lax.all_gather(out_weight, 'ctx', axis=1, tiled=True)]
    all_to_all x0 -> x1, starting transfers between devices: none -> 8.78 us  [local(): lax.all_to_all(jnp.stack([out_weight] * lax.axis_size('ctx')), 'ctx', 0, 0)]
    another operation x0 -> x1, local copies, waits for them, and re-layouts: none -> 4.16 us  [local(): jnp.stack([out_weight] * lax.axis_size('ctx'))]
  transfers between devices with their start and end apart: 3 -> 3, of which waited for: 2 -> 1; matrix products, arithmetic and copies ran while one was open for 13% -> 11% of each run, Pallas kernels for 0% -> 0%
where the time goes in v1:
time: 334 us
  blocking collectives  162 us (49%)
  waiting for transfers between devices  93.1 us (28%)
  matrix products  31.4 us (9%)
  between operations  14.3 us (4%)
  other arithmetic  12.2 us (4%)
  local copies, waits for them, and re-layouts  11.3 us (3%)
  starting transfers between devices  8.82 us (3%)
    unnamed x1, blocking collectives  162 us
    reduce_scatter x1, waiting for transfers between devices, local(): lax.psum_scatter(projected.astype(jnp.bfloat16), 'head', scatter_dimensio...  93.1 us
    dot_general x1, matrix products, local(): jnp.dot(flattened, jnp.concatenate(lax.all_to_all(jnp.stack([out_weight]...  10.2 us
    all_to_all x1, starting transfers between devices, local(): lax.all_to_all(jnp.stack([out_weight] * lax.axis_size('ctx')), 'ctx', 0, 0)  8.78 us
  transfers between devices with their start and end apart: 3, of which 1 were waited for; matrix products, arithmetic and copies ran while one was open for 11% of the time, Pallas kernels for 0%

profile of v1, /device:TPU:1, one launch (start us, length us, event | category | flops | bytes accessed | tf_op | source)
XLA Modules:
  0.0 333.7 jit_solution(12239890990105695395)
XLA Ops:
  6.5 0.8 reshape.173
  7.3 1.2 reduce_window_sum.37
  9.2 1.2 reshape.176
  10.4 1.2 reshape.175
  12.2 2.4 fusion.17
  14.6 0.7 convert_element_type.45
  15.5 4.2 %stack.2 = bf16[32,512,256]{1,2,0:T(8,128)(2,1)} broadcast(bf16[512,256]{0,1:T(8,128)(2,1)S(1)} %copy.51), dimensions={1,2} | broadcast | bytes 8650752 | tf_op jit(solution)/shard_map/stack | solution.py:129
  19.6 8.8 %all-to-all-start = ((bf16[32,512,256]{1,2,0:T(8,128)(2,1)}), bf16[32,512,256]{1,2,0:T(8,128)(2,1)}, u32[]{:S(2)}, u32[]{:S(2)}) async-start(bf16[32,512,256]{1,2,0:T(8,128)(2,1)} %stack.2), calls=%async_computation | async-start | bytes 16777216 | tf_op jit(solution)/shard_map/all_to_all | solution.py:129
  30.1 162.5 %all-reduce = f32[128]{0:T(128)S(1)} all-reduce(f32[128]{0:T(128)S(1)} %dynamic-update-slice), channel_id=3, replica_groups=mesh['ctx'=32,'head'=8] {'ctx'}, use_global_device_ids=true, to_apply=%add | all-reduce | flops 128 | bytes 1024
  194.0 3.2 fusion.7
  197.2 3.2 fusion.8
  200.4 2.9 multiply_convert_fusion
  203.3 6.6 %fusion.4 = f32[5,4,128,128]{3,0,2,1:T(8,128)S(1)} fusion(bf16[32,4,128,128]{3,2,1,0:T(8,128)(2,1)} %bitcast.68, f32[32,4]{0,1:T(4,128)S(1)} %copy.46, pred[5,32]{1,0:T(8,128)(4,1)S(1)} %fusion.55), kind=kOutput, calls=%fused_computation.6 | convolution fusion | flops 125829760 | bytes 5505696 | tf_op jit(solution)/shard_map/jnh,nhde->jhde/dot_general | solution.py:98
  209.9 1.2 fusion.63
  211.1 1.1 fusion.21
  212.2 1.1 fusion.22
  213.2 1.1 fusion.23
  214.3 1.0 fusion.24
  215.4 1.1 fusion.25
  216.4 3.4 %fusion.2 = f32[4,4,128,128]{2,3,1,0:T(8,128)S(1)} fusion(bf16[4,4,128,896]{2,3,1,0:T(8,128)(2,1)S(1)} %bitcast.67, bf16[4,4,896,128]{3,1,2,0:T(4,128)(2,1)} %fusion.25), kind=kOutput, calls=%fused_computation.4 | convolution fusion | flops 469762048 | bytes 8388608 | tf_op jit(solution)/shard_map/hctk,hcke->hcte/dot_general | solution.py:118
  219.8 2.1 multiply_reduce_fusion
  221.9 1.3 fusion.10
  223.6 10.2 %convolution_convert_fusion = bf16[512,8192]{1,0:T(8,128)(2,1)} fusion(bf16[512,8192]{0,1:T(8,128)(2,1)} %bitcast.32, bf16[64,8,4,128]{3,2,1,0:T(4,128)(2,1)S(1)} %bitcast.75), kind=kOutput, calls=%fused_computation | convolution fusion | flops 4299161600 | bytes 17301504 | tf_op jit(solution)/shard_map/dot_general | solution.py:126
  233.8 93.1 %reduce-scatter.2.cloned.1.call-done = bf16[512,1024]{1,0:T(8,128)(2,1)} async-done(((bf16[512,8192]{1,0:T(8,128)(2,1)}), bf16[512,1024]{1,0:T(8,128)(2,1)}) %reduce-scatter.2.cloned.1.call-update) | async-done | bytes 1048592 | tf_op jit(solution)/shard_map/reduce_scatter | solution.py:133
  (56 shorter events, 4.2 us)
Async XLA Ops:
  6.5 186.3 %copy-start = (f32[4,8,16]{2,1,0:T(8,128)S(1)}, f32[4,8,16]{2,1,0:T(8,128)}, u32[]{:S(2)}) copy-start(f32[4,8,16]{2,1,0:T(8,128)} %param.14) | copy-start | bytes 6148
  6.5 8.8 %copy-start.4 = (bf16[512,256]{1,0:T(8,128)(2,1)S(1)}, bf16[512,256]{1,0:T(8,128)(2,1)}, u32[]{:S(2)}) copy-start(bf16[512,256]{1,0:T(8,128)(2,1)} %param.15) | copy-start | bytes 786436
  6.5 196.8 %all-gather.4.cloned.1.call-start = ((), (), s32[]{:S(2)}) async-start(), calls=%async_computation.3 | async-start | bytes 4325376 | tf_op jit(solution)/shard_map/all_gather | solution.py:83
  19.6 9.0 %copy-start.7 = (u32[256]{0:T(256)S(1)}, u32[256]{0:T(256)}, u32[]{:S(2)}) copy-start(u32[256]{0:T(256)} %constant.43) | copy-start | bytes 3076
  19.6 173.3 %copy-start.5 = (s32[4,512]{1,0:T(4,128)S(1)}, s32[4,512]{1,0:T(4,128)}, u32[]{:S(2)}) copy-start(s32[4,512]{1,0:T(4,128)} %param.13) | copy-start | bytes 24580
  19.6 173.4 %copy-start.2 = (bf16[512,512]{1,0:T(8,128)(2,1)S(1)}, bf16[512,512]{1,0:T(8,128)(2,1)}, u32[]{:S(2)}) copy-start(bf16[512,512]{1,0:T(8,128)(2,1)} %param.9) | copy-start | bytes 1572868
  19.6 203.9 %all-to-all-start = ((bf16[32,512,256]{1,2,0:T(8,128)(2,1)}), bf16[32,512,256]{1,2,0:T(8,128)(2,1)}, u32[]{:S(2)}, u32[]{:S(2)}) async-start(bf16[32,512,256]{1,2,0:T(8,128)(2,1)} %stack.2), calls=%async_computation | async-start | bytes 16777216 | tf_op jit(solution)/shard_map/all_to_all | solution.py:129
  28.4 165.6 %copy-start.8 = (pred[4,4]{1,0:T(4,128)(4,1)S(1)}, pred[4,4]{1,0:T(4,128)(4,1)}, u32[]{:S(2)}) copy-start(pred[4,4]{1,0:T(4,128)(4,1)} %constant.36.clone) | copy-start | bytes 52
  28.4 168.7 %copy-start.6 = (pred[4,4]{1,0:T(4,128)(4,1)S(1)}, pred[4,4]{1,0:T(4,128)(4,1)}, u32[]{:S(2)}) copy-start(pred[4,4]{1,0:T(4,128)(4,1)} %constant.37.clone) | copy-start | bytes 52
  28.4 298.4 %reduce-scatter.2.cloned.1.call-start = ((), (), s32[]{:S(2)}) async-start(), calls=%async_computation.2 | async-start | bytes 9437184 | tf_op jit(solution)/shard_map/reduce_scatter | solution.py:133
  193.1 10.3 %copy-start.3 = (f32[4,8,4,128]{3,1,2,0:T(8,128)}, f32[4,8,4,128]{3,1,2,0:T(8,128)S(1)}, u32[]{:S(2)}) copy-start(f32[4,8,4,128]{3,1,2,0:T(8,128)S(1)} %convolution_bitcast_fusion) | copy-start | bytes 196612
  209.9 6.5 %copy-start.1 = (bf16[4,4,128,7,128]{2,4,3,1,0:T(8,128)(2,1)S(1)}, bf16[4,4,128,7,128]{2,4,3,1,0:T(8,128)(2,1)}, u32[]{:S(2)}) copy-start(bf16[4,4,128,7,128]{2,4,3,1,0:T(8,128)(2,1)} %multiply_convert_fusion) | copy-start | bytes 11010052
  216.4 3.4 %slice-start = ((f32[4,8,4,128]{3,1,2,0:T(8,128)}), f32[4,1,4,128]{3,1,2,0:T(1,128)S(1)}, s32[]{:S(2)}) async-start(f32[4,8,4,128]{3,1,2,0:T(8,128)} %copy-done.3), calls=%async_computation.4 | async-start | bytes 16384 | tf_op jit(solution)/shard_map/slice | solution.py:37
Sparse Core Ops, SparseCore 0:
  15.4 121.6 all-gather.3
  233.9 92.8 reduce-scatter.1
